TPU v7x, 32 devices: a whole 2x2x4 slice. The times are simulated.
32 devices in a mesh: grp: 2 (over y), patch: 4 (over z), sub: 2 (over x), pair: 2 (over core).
Axes of the slice: x: 2, y: 2, z: 4, core: 2. Of those that a mesh axis runs over, the one named last changes fastest.
Arguments:
- positions: float32 [1024, 3, 768], P(('grp', 'patch')), parts along dimension 0, may hold values from -6 to 6
- drive: float32 [1024, 3, 768], P(('grp', 'patch')), parts along dimension 0, may hold values from -6 to 6
- history: float32 [1024, 3, 768], P(('grp', 'patch', 'sub'), None, 'pair'), parts along dimension 0, may hold values from -6 to 6
- hist_dest: int32 [1024], P(('grp', 'patch', 'sub')), parts along dimension 0, may hold values from 0 to 511, as said below
- tile_target: int32 [384], P(('grp', 'patch', 'sub')), parts along dimension 0, may hold values from 0 to 127, as said below
- tile_source: int32 [384], P(('grp', 'patch', 'sub')), parts along dimension 0, may hold values from 0 to 383
- tile_count: int32 [16], P(('grp', 'patch', 'sub')), parts along dimension 0, may hold values from 1 to 24, as said below
Outputs:
- velocity: float32 [1024, 3, 768], P(('grp', 'patch', 'sub'), None, 'pair'), parts along dimension 0
- new_positions: float32 [1024, 3, 768], P(('grp', 'patch', 'sub'), None, 'pair'), parts along dimension 0
There are 2 independent parts, one for each index of `grp`. A program takes and returns all parts, laid end to end along the dimension named above; each array names one. Nothing has to cross between parts.
Inputs may be any that keep to these rules, and one draw needn't show every extreme that they name: `tile_target`: target and source pairs of one patch's 2 * 24 slots are distinct. `tile_count`: in every draw some patch has 24 live slots in all its lists. `hist_dest`: A permutation of the panels in which dest % 128 equals the former panel's index % 128: a panel keeps its place in its block of 64, only the patch changes. The 64 panels of one block go to at most 16 per patch, a bound reached in every draw, and every block receives one panel for each place.
All inputs are finite; a program needn't handle non-finite values.
Results may differ from a plain program's by a relative error of at most 0.0003.
Values sent between devices are 32-bit elements; how exact they have to be, the bound alone decides.
A program may use at most 64 MiB of HBM per device.

v0:
```python
import functools
import math

import jax
import jax.numpy as jnp
from jax import lax
from jax.experimental import pallas as pl
from jax.experimental.pallas import tpu as pltpu
from jax.sharding import PartitionSpec as P

PTS = 96
EPSILON_SQ = 0.0625
SCALE_8PI = 1.0 / (8.0 * math.pi)
STIFFNESS = 0.25
CHUNK = 768
GROUP = 4

VMEM = pl.BlockSpec(memory_space=pltpu.VMEM)
SMEM = pl.BlockSpec(memory_space=pltpu.SMEM)


def cilium_forces(points, drive):
    width = points.shape[1]
    place = lax.broadcasted_iota(jnp.int32, points.shape, 1) % PTS
    before = jnp.where(place == 0, points, pltpu.roll(points, 1, 1))
    after = jnp.where(place == PTS - 1, points, pltpu.roll(points, width - 1, 1))
    return STIFFNESS * (before + after - 2.0 * points) + drive


def half_at(side, half):
    return pl.ds(pl.multiple_of(side * half, 128), half)


def rows_at(ref, index, lanes=slice(None), first=0):
    return jnp.concatenate(
        [ref[c, pl.ds(index, 1), lanes] for c in range(first, first + 3)], axis=0
    )


def pack_history_kernel(panels, info_ref, dest_ref, hist_ref, out_ref, taken):
    patches = out_ref.shape[0]
    me = info_ref[0]
    for o in range(patches):
        taken[o] = 0

    def one(b, carry):
        owner = dest_ref[b] // panels
        rel = lax.rem(owner - me + patches, patches)
        row = taken[rel]
        taken[rel] = row + 1
        for c in range(3):
            out_ref[rel, c, pl.ds(row, 1), :] = hist_ref[c, pl.ds(b, 1), :]
        return carry

    lax.fori_loop(0, hist_ref.shape[1], one, 0)


def pack_near_kernel(slots, info_ref, left_ref, right_ref, pos_ref, drive_ref, to_left, to_right):
    panels = pos_ref.shape[1]
    half = to_left.shape[2]
    lanes = half_at(info_ref[2], half)

    def one(i, msg_ref, out_ref, first):
        wanted = msg_ref[i] - first

        @pl.when((wanted >= 0) & (wanted < panels) & (i < msg_ref[slots]))
        def _():
            points = rows_at(pos_ref, wanted, lanes)
            forces = cilium_forces(points, rows_at(drive_ref, wanted, lanes))
            for c in range(3):
                out_ref[c, pl.ds(i, 1), :] = points[c : c + 1]
                out_ref[3 + c, pl.ds(i, 1), :] = forces[c : c + 1]

    def both(i, carry):
        one(i, right_ref, to_right, 0)
        one(i, left_ref, to_left, 2 * panels)
        return carry

    lax.fori_loop(0, slots, both, 0)


def split3(value):
    high = value.astype(jnp.bfloat16).astype(jnp.float32)
    rest = value - high
    middle = rest.astype(jnp.bfloat16).astype(jnp.float32)
    return high, middle, rest - middle


def tile_velocity(target, sources):
    center = jnp.mean(target, axis=1, keepdims=True)
    x = target - center
    width = x.shape[1]
    xx = jnp.sum(x * x, axis=0, keepdims=True)
    ones = jnp.ones((1, width), jnp.float32)
    none = jnp.zeros((3, width), jnp.float32)
    qh, qm, ql = split3(jnp.concatenate([-2.0 * x, ones, xx + EPSILON_SQ, none], axis=0))
    right = jnp.concatenate([qh, qm, qh, qm, ql, qh], axis=0).astype(jnp.bfloat16)
    total = small = None
    for points, force in sources:
        y = points - center
        length = y.shape[1]
        yy = jnp.sum(y * y, axis=0, keepdims=True)
        yf = jnp.sum(y * force, axis=0, keepdims=True)
        ones = jnp.ones((1, length), jnp.float32)
        none = jnp.zeros((3, length), jnp.float32)
        ph, pm, pw = split3(jnp.concatenate([y, yy, ones, none], axis=0))
        left = jnp.concatenate([ph, ph, pm, pm, ph, pw], axis=0).astype(jnp.bfloat16)
        pad = jnp.zeros((5, length), jnp.float32)
        weights = jnp.concatenate(
            [force, yf, force * y[0:1], yf * y[0:1], force * y[1:2], yf * y[1:2],
             force * y[2:3], yf * y[2:3], force * yy, pad],
            axis=0,
        )
        weights = jnp.concatenate(split3(weights), axis=0).astype(jnp.bfloat16)
        tail_rows = 2 * weights.shape[0] // 3
        for start in range(0, length, CHUNK):
            stop = min(start + CHUNK, length)
            squared = lax.dot_general(
                left[:, start:stop], right, (((0,), (0,)), ((), ())),
                preferred_element_type=jnp.float32,
            )
            inverse = lax.rsqrt(squared)
            cube = inverse * inverse * inverse
            high = cube.astype(jnp.bfloat16)
            low = (cube - high.astype(jnp.float32)).astype(jnp.bfloat16)
            some = weights[:, start:stop]
            part = jnp.dot(some, high, preferred_element_type=jnp.float32)
            tail = jnp.dot(some[:tail_rows], low, preferred_element_type=jnp.float32)
            total = part if total is None else total + part
            small = tail if small is None else small + tail
    rows = total.shape[0] // 3
    total = total[2 * rows :] + small[rows:] + total[rows : 2 * rows] + small[:rows] + total[:rows]
    plain, along = total[0:3], total[3:4]
    by_y = [total[4 + 4 * c : 7 + 4 * c] for c in range(3)]
    along_y = [total[7 + 4 * c : 8 + 4 * c] for c in range(3)]
    lengths = total[16:19]
    direct = (xx + 2.0 * EPSILON_SQ) * plain + lengths
    for c in range(3):
        direct = direct - 2.0 * x[c : c + 1] * by_y[c]
    shared = jnp.sum(x * plain, axis=0, keepdims=True) - along
    outs = []
    for c in range(3):
        outs.append(
            SCALE_8PI
            * (
                direct[c : c + 1]
                + x[c : c + 1] * shared
                - jnp.sum(x * by_y[c], axis=0, keepdims=True)
                + along_y[c]
            )
        )
    return outs


def each_slot(chosen, count, wanted, work):
    def note(i, found):
        chosen[found] = i
        return found + wanted(i).astype(jnp.int32)

    found = lax.fori_loop(0, count, note, 0)

    def group(j, carry):
        for k in range(GROUP):
            work(chosen[jnp.minimum(j * GROUP + k, found - 1)])
        return carry

    lax.fori_loop(0, (found + GROUP - 1) // GROUP, group, 0)


def own_tiles_kernel(info_ref, source_ref, target_ref, count_ref, pos_ref, drive_ref, out_ref, chosen):
    panels = pos_ref.shape[1]
    half = out_ref.shape[2]
    lanes = half_at(info_ref[2], half)

    def wanted(i):
        return source_ref[i] // panels == 1

    def work(i):
        source = source_ref[i] - panels
        points = rows_at(pos_ref, source)
        forces = cilium_forces(points, rows_at(drive_ref, source))
        rows = tile_velocity(rows_at(pos_ref, target_ref[i], lanes), [(points, forces)])
        for c in range(3):
            out_ref[c, pl.ds(i, 1), :] = rows[c]

    each_slot(chosen, count_ref[0], wanted, work)


def near_tiles_kernel(
    info_ref, source_ref, target_ref, count_ref, pos_ref, lefta, leftb, righta, rightb, own_ref,
    out_ref, chosen
):
    panels = pos_ref.shape[1]
    half = out_ref.shape[2]
    lanes = half_at(info_ref[2], half)
    out_ref[...] = own_ref[...]

    def wanted(i):
        return source_ref[i] // panels != 1

    def work(i):
        is_left = source_ref[i] < panels

        def both(first):
            return jnp.concatenate(
                [
                    jnp.where(is_left, rows_at(a, i, first=first), rows_at(b, i, first=first))
                    for a, b in ((lefta, righta), (leftb, rightb))
                ],
                axis=1,
            )

        rows = tile_velocity(rows_at(pos_ref, target_ref[i], lanes), [(both(0), both(3))])
        for c in range(3):
            out_ref[c, pl.ds(i, 1), :] = rows[c]

    each_slot(chosen, count_ref[0], wanted, work)


def base_kernel(patches, *refs):
    info_ref = refs[0]
    dests = refs[1 : 1 + patches]
    pos_ref, packed_ref = refs[1 + patches : 3 + patches]
    arrived = refs[3 + patches : 2 + 2 * patches]
    out_ref, places = refs[-2:]
    blocks, half = out_ref.shape[1:]
    panels = pos_ref.shape[1]
    me, side = info_ref[0], info_ref[2]
    first = pl.multiple_of(info_ref[1] * blocks, blocks)
    for shift in range(patches):
        old_ref = packed_ref.at[0] if shift == 0 else arrived[shift - 1]

        def note(b, found, shift=shift):
            places[found] = b
            return found + (dests[shift][b] // panels == me).astype(jnp.int32)

        found = lax.fori_loop(0, blocks, note, 0, unroll=8)

        def put(r, carry, old_ref=old_ref):
            for c in range(3):
                out_ref[c, pl.ds(places[r], 1), :] = old_ref[c, pl.ds(r, 1), :]
            return carry

        lax.fori_loop(0, found, put, 0)
    mine = pos_ref[:, pl.ds(first, blocks), half_at(side, half)]
    out_ref[...] = (4.0 * mine - out_ref[...]) / 3.0


def finish_kernel(subs, slots, *refs):
    info_ref = refs[0]
    lists = refs[1 : 1 + subs]
    shares = refs[1 + subs : 1 + 2 * subs]
    base_ref, vel_ref, new_ref = refs[1 + 2 * subs :]
    blocks = vel_ref.shape[1]
    first = info_ref[1] * blocks
    vel_ref[...] = jnp.zeros_like(vel_ref)
    for list_ref, share_ref in zip(lists, shares):

        def add(i, carry, list_ref=list_ref, share_ref=share_ref):
            place = list_ref[i] - first

            @pl.when((place >= 0) & (place < blocks))
            def _():
                for c in range(3):
                    vel_ref[c, pl.ds(place, 1), :] += share_ref[c, pl.ds(i, 1), :]

            return carry

        lax.fori_loop(0, list_ref[slots], add, 0)
    new_ref[...] = base_ref[...] + (1.0 / 3.0) * vel_ref[...]


def local(positions, drive, history, hist_dest, tile_target, tile_source, tile_count):
    panels = positions.shape[0]
    panel_len = positions.shape[2]
    patches, subs, pairs = (lax.axis_size(a) for a in ("patch", "sub", "pair"))
    half = panel_len // pairs
    slots = tile_target.shape[0]
    blocks = history.shape[0]
    per_peer = (blocks + patches - 1) // patches
    info = jnp.stack(
        [lax.axis_index("patch"), lax.axis_index("sub"), lax.axis_index("pair")]
    ).astype(jnp.int32)
    f32 = jnp.float32
    params = pltpu.CompilerParams(vmem_limit_bytes=48 * 1024 * 1024)
    positions, drive, history = (jnp.transpose(a, (1, 0, 2)) for a in (positions, drive, history))

    def shifted(value, axis, shift):
        count = lax.axis_size(axis)
        return lax.ppermute(value, axis, [(i, (i + shift) % count) for i in range(count)])

    message = jnp.concatenate([tile_source, tile_count, hist_dest])
    heard = [message] + [shifted(message, "patch", s) for s in range(1, patches)]
    targets = jnp.concatenate([tile_target, tile_count])
    lists = [targets] + [shifted(targets, "sub", s) for s in range(1, subs)]

    packed = pl.pallas_call(
        functools.partial(pack_history_kernel, panels),
        out_shape=jax.ShapeDtypeStruct((patches, 3, per_peer, half), f32),
        in_specs=[SMEM, SMEM, VMEM],
        out_specs=VMEM,
        scratch_shapes=[pltpu.SMEM((patches,), jnp.int32)],
        compiler_params=params,
        name="pack_history",
    )(info, hist_dest, history)
    packed, *heard = lax.optimization_barrier((packed, *heard))
    dests = [hist_dest] + [m[slots + 1 :] for m in heard[1:]]

    near = jax.ShapeDtypeStruct((6, slots, half), f32)
    to_left, to_right = pl.pallas_call(
        functools.partial(pack_near_kernel, slots),
        out_shape=(near, near),
        in_specs=[SMEM, SMEM, SMEM, VMEM, VMEM],
        out_specs=(VMEM, VMEM),
        compiler_params=params,
        name="pack_near",
    )(info, heard[1], heard[-1], positions, drive)

    up = [(i, i + 1) for i in range(patches - 1)]
    from_left = lax.ppermute(to_right, "patch", up)
    from_right = lax.ppermute(to_left, "patch", [(b, a) for a, b in up])

    arrived = [shifted(packed[s], "patch", s) for s in range(1, patches)]

    tiles = jax.ShapeDtypeStruct((3, slots, half), f32)
    chosen = [pltpu.SMEM((slots + 1,), jnp.int32)]
    pairs_all = slots * half * panel_len
    cost = pl.CostEstimate(
        flops=pairs_all * 256, bytes_accessed=4 * positions.size * 2, transcendentals=pairs_all
    )
    own = pl.pallas_call(
        own_tiles_kernel,
        out_shape=tiles,
        in_specs=[SMEM] * 4 + [VMEM] * 2,
        out_specs=VMEM,
        scratch_shapes=chosen,
        compiler_params=params,
        cost_estimate=cost,
        name="own_tiles",
    )(info, tile_source, tile_target, tile_count, positions, drive)

    other_left = shifted(from_left, "pair", 1)
    other_right = shifted(from_right, "pair", 1)
    share = pl.pallas_call(
        near_tiles_kernel,
        out_shape=tiles,
        in_specs=[SMEM] * 4 + [VMEM] * 6,
        out_specs=VMEM,
        scratch_shapes=chosen,
        compiler_params=params,
        cost_estimate=cost,
        name="near_tiles",
    )(info, tile_source, tile_target, tile_count, positions,
      from_left, other_left, from_right, other_right, own)
    shares = [share] + [shifted(share, "sub", s) for s in range(1, subs)]
    _, *arrived = lax.optimization_barrier((share, *arrived))

    out = jax.ShapeDtypeStruct((3, blocks, half), f32)
    base = pl.pallas_call(
        functools.partial(base_kernel, patches),
        out_shape=out,
        in_specs=[SMEM] * (1 + patches) + [VMEM] * (1 + patches),
        out_specs=VMEM,
        scratch_shapes=[pltpu.SMEM((blocks + 1,), jnp.int32)],
        compiler_params=params,
        name="base",
    )(info, *dests, positions, packed, *arrived)
    outs = pl.pallas_call(
        functools.partial(finish_kernel, subs, slots),
        out_shape=(out, out),
        in_specs=[SMEM] * (1 + subs) + [VMEM] * (1 + subs),
        out_specs=(VMEM, VMEM),
        compiler_params=params,
        name="finish",
    )(info, *lists, *shares, base)
    return tuple(jnp.transpose(a, (1, 0, 2)) for a in outs)


def solution(mesh):
    by_list = P(("grp", "patch", "sub"))
    halves = P(("grp", "patch", "sub"), None, "pair")
    whole = P(("grp", "patch"), None, None)
    return jax.shard_map(
        local,
        mesh=mesh,
        in_specs=(whole, whole, halves, by_list, by_list, by_list, by_list),
        out_specs=(halves, halves),
        check_vma=False,
    )
```

profile of v0, /device:TPU:28, one launch (start us, length us, event | category | flops | bytes accessed | tf_op | source)
XLA Modules:
  0.0 48.7 jit_solution(13457202918327121925)
XLA Ops:
  1.3 0.7 %pad_add_fusion.2 = s32[89]{0:T(128)S(1)} fusion(s32[64]{0:T(128)} %refs_1_.1, s32[1]{0:T(128)S(6)} %copy.9.count_ref, s32[24]{0:T(128)} %source_ref.3), kind=kLoop, calls=%fused_computation.5 | loop fusion | flops 178 | bytes 712 | tf_op jit(solution)/shard_map/concatenate | solution.py:292
  2.0 0.2 collective-permute-start.1
  2.2 1.7 %collective-permute-start.2 = (s32[89]{0:T(128)S(1)}, s32[89]{0:T(128)S(1)}, u32[]{:S(2)}, u32[]{:S(2)}) collective-permute-start(s32[89]{0:T(128)S(1)} %pad_add_fusion.2), channel_id=1, source_target_pairs={{0,8},{4,12},{8,0},{12,4},{1,9},{5,13},{9,1},{13,5},{2,10},{6,14},... | collective-permute-start | bytes 1076 | tf_op jit(solution)/shard_map/ppermute | solution.py:290
  3.9 0.4 collective-permute-start.3
  4.4 0.1 pad_add_fusion.info_ref.refs_0_
  4.5 0.0 copy-start.4
  4.5 1.0 %copy-done.4 = f32[64,3,384]{2,0,1:T(8,128)S(1)} copy-done((f32[64,3,384]{2,0,1:T(8,128)S(1)}, f32[64,3,384]{2,0,1:T(8,128)}, u32[]{:S(2)}) %copy-start.4) | copy-done | bytes 294936
  5.4 0.0 copy-start.5
  5.4 0.7 %copy-done.5 = s32[64]{0:T(128)S(1)} copy-done((s32[64]{0:T(128)S(1)}, s32[64]{0:T(128)}, u32[]{:S(2)}) %copy-start.5) | copy-done | bytes 280
  6.1 1.9 %pack_history.1.refs_6_ = f32[4,3,16,384]{3,2,1,0:T(8,128)S(1)} custom-call(s32[3]{0:T(128)S(1)} %pad_add_fusion.info_ref.refs_0_, s32[64]{0:T(128)S(1)} %copy-done.5, f32[3,64,384]{2,1,0:T(8,128)S(1)} %bitcast.20), custom_call_target="tpu_custom_call" | custom-call | tf_op jit(solution)/shard_map/pack_history/pallas_call | solution.py:297
  8.0 0.0 collective-permute-done.1.left_ref
  8.0 0.0 collective-permute-done.2
  8.0 1.3 %collective-permute-done.3.right_ref = s32[89]{0:T(128)S(1)} collective-permute-done((s32[89]{0:T(128)S(1)}, s32[89]{0:T(128)S(1)}, u32[]{:S(2)}, u32[]{:S(2)}) %collective-permute-start.3) | collective-permute-done | bytes 388 | tf_op jit(solution)/shard_map/ppermute | solution.py:290
  9.3 0.0 copy-start
  9.3 1.3 %copy-done = f32[128,3,768]{2,0,1:T(8,128)S(1)} copy-done((f32[128,3,768]{2,0,1:T(8,128)S(1)}, f32[128,3,768]{2,0,1:T(8,128)}, u32[]{:S(2)}) %copy-start) | copy-done | bytes 1179672
  10.6 0.0 copy-start.2
  10.6 1.3 %copy-done.2 = f32[128,3,768]{2,0,1:T(8,128)S(1)} copy-done((f32[128,3,768]{2,0,1:T(8,128)S(1)}, f32[128,3,768]{2,0,1:T(8,128)}, u32[]{:S(2)}) %copy-start.2) | copy-done | bytes 1179672
  11.8 1.5 %pack_near.1 = (f32[6,24,384]{2,1,0:T(8,128)S(1)}, f32[6,24,384]{2,1,0:T(8,128)S(1)}) custom-call(s32[3]{0:T(128)S(1)} %pad_add_fusion.info_ref.refs_0_, s32[89]{0:T(128)S(1)} %collective-permute-done.1.left_ref, s32[89]{0:T(128)S(1)} %collective-permute-done.3.right_ref, f32[3,128,768]{2,1,0:T(8,128)S(1)} %bitcast.14, f32[3,128,768]{2,1,0:T(8,128)S(1)} %bitcast.18), custom_call_target="tpu_custom_call" | custom-call | tf_op jit(solution)/shard_map/pack_near/pallas_call | solution.py:310
  13.3 1.3 %collective-permute-start.4 = (f32[6,24,384]{2,1,0:T(8,128)S(1)}, f32[6,24,384]{2,1,0:T(8,128)S(1)}, u32[]{:S(2)}, u32[]{:S(2)}) collective-permute-start(f32[6,24,384]{2,1,0:T(8,128)S(1)} %get-tuple-element.15), channel_id=1, source_target_pairs={{0,4},{4,8},{8,12},{1,5},{5,9},{9,13},{2,6},{6,10},{10,14},{3,7},{... | collective-permute-start | bytes 663560 | tf_op jit(solution)/shard_map/ppermute | solution.py:320
  14.6 4.6 %collective-permute-start.6 = (f32[6,24,384]{2,1,0:T(8,128)S(1)}, f32[6,24,384]{2,1,0:T(8,128)S(1)}, u32[]{:S(2)}, u32[]{:S(2)}) collective-permute-start(f32[6,24,384]{2,1,0:T(8,128)S(1)} %get-tuple-element.16), channel_id=1, source_target_pairs={{4,0},{8,4},{12,8},{5,1},{9,5},{13,9},{6,2},{10,6},{14,10},{7,3},{... | collective-permute-start | bytes 663560 | tf_op jit(solution)/shard_map/ppermute | solution.py:321
  19.2 0.0 copy-done.1
  19.2 0.0 copy-done.3
  19.2 0.0 copy-done.6
  19.2 0.0 copy-done.7
  19.3 7.5 %own_tiles.1.own_ref = f32[3,24,384]{2,1,0:T(8,128)S(1)} custom-call(s32[3]{0:T(128)S(1)} %pad_add_fusion.info_ref.refs_0_, s32[24]{0:T(128)S(1)} %copy-done.6, s32[24]{0:T(128)S(1)} %copy-done.7, s32[1]{0:T(128)S(6)} %copy.9.count_ref, f32[3,128,768]{2,1,0:T(8,128)S(1)} %bitcast.15, f32[3,128,768]{2,1,0:T(8,128)S(1)} %bitcast.19), custom_call_target="tpu_custom_call" | custom-call | flops 1811939328 | bytes 2359296 | tf_op jit(solution)/shard_map/own_tiles/pallas_call | solution.py:331
  26.7 0.0 collective-permute-done.4.lefta
  26.7 0.1 collective-permute-start.5
  26.8 0.0 collective-permute-done.6.righta
  26.8 0.5 %collective-permute-start.7 = (f32[6,24,384]{2,1,0:T(8,128)S(1)}, f32[6,24,384]{2,1,0:T(8,128)S(1)}, u32[]{:S(2)}, u32[]{:S(2)}) collective-permute-start(f32[6,24,384]{2,1,0:T(8,128)S(1)} %collective-permute-done.6.righta), channel_id=1, source_target_pairs={{0,1},{1,0},{2,3},{3,2},{4,5},{5,4},{6,7},{7,6},{8,9},{9,8},{10,11... | collective-permute-start | bytes 663560 | tf_op jit(solution)/shard_map/ppermute | solution.py:290
  27.3 0.1 collective-permute-start.10
  27.4 0.1 collective-permute-start.11
  27.5 3.8 %collective-permute-start.9 = (f32[3,16,384]{2,1,0:T(8,128)S(1)}, f32[3,16,384]{2,1,0:T(8,128)S(1)}, u32[]{:S(2)}, u32[]{:S(2)}) collective-permute-start(f32[3,16,384]{2,1,0:T(8,128)S(1)} %get-tuple-element.26), channel_id=1, source_target_pairs={{0,4},{4,8},{8,12},{12,0},{1,5},{5,9},{9,13},{13,1},{2,6},{6,10},{... | collective-permute-start | bytes 221192 | tf_op jit(solution)/shard_map/ppermute | solution.py:290
  31.3 0.0 collective-permute-done.5.leftb
  31.3 0.0 collective-permute-done.7.rightb
  31.3 9.7 %near_tiles.1.refs_3_ = f32[3,24,384]{2,1,0:T(8,128)S(1)} custom-call(s32[3]{0:T(128)S(1)} %pad_add_fusion.info_ref.refs_0_, s32[24]{0:T(128)S(1)} %copy-done.6, s32[24]{0:T(128)S(1)} %copy-done.7, s32[1]{0:T(128)S(6)} %copy.9.count_ref, f32[3,128,768]{2,1,0:T(8,128)S(1)} %bitcast.16, f32[6,24,384]{2,1,0:T(8,128)S(1)} %collective-permute-done.4.lefta, ...), custom_call_target="tpu_custom_call" | custom-call | flops 1811939328 | bytes 2359296 | tf_op jit(solution)/shard_map/near_tiles/pallas_call | solution.py:344
  41.0 0.1 collective-permute-start.8
  41.1 0.1 pad_add_fusion.1.refs_1_
  41.1 2.0 %collective-permute-start = (s32[25]{0:T(128)S(1)}, s32[25]{0:T(128)S(1)}, u32[]{:S(2)}, u32[]{:S(2)}) collective-permute-start(s32[25]{0:T(128)S(1)} %pad_add_fusion.1.refs_1_), channel_id=1, source_target_pairs={{0,2},{2,0},{1,3},{3,1},{4,6},{6,4},{5,7},{7,5},{8,10},{10,8},{9,1... | collective-permute-start | bytes 308 | tf_op jit(solution)/shard_map/ppermute | solution.py:290
  43.1 0.1 slice.18.refs_2_
  43.2 0.1 slice.20.refs_4_
  43.3 0.1 slice.19.refs_3_
  43.4 0.0 collective-permute-done.10.refs_8_
  43.4 0.0 collective-permute-done.11.refs_9_
  43.4 0.0 collective-permute-done.9.refs_7_
  43.4 3.1 %base.1.refs_5_ = f32[3,64,384]{2,1,0:T(8,128)S(1)} custom-call(s32[3]{0:T(128)S(1)} %pad_add_fusion.info_ref.refs_0_, s32[64]{0:T(128)S(1)} %copy-done.5, s32[64]{0:T(128)S(1)} %slice.18.refs_2_, s32[64]{0:T(128)S(1)} %slice.19.refs_3_, s32[64]{0:T(128)S(1)} %slice.20.refs_4_, f32[3,128,768]{2,1,0:T(8,128)S(1)} %bitcast.17, ...), custom_call_target="tpu_custom_call" | custom-call | tf_op jit(solution)/shard_map/base/pallas_call | solution.py:359
  46.5 0.0 collective-permute-done.refs_2_
  46.5 0.0 collective-permute-done.8.refs_4_
  46.5 2.2 %finish.1 = (f32[3,64,384]{2,1,0:T(8,128)}, f32[3,64,384]{2,1,0:T(8,128)}) custom-call(s32[3]{0:T(128)S(1)} %pad_add_fusion.info_ref.refs_0_, s32[25]{0:T(128)S(1)} %pad_add_fusion.1.refs_1_, s32[25]{0:T(128)S(1)} %collective-permute-done.refs_2_, f32[3,24,384]{2,1,0:T(8,128)S(1)} %near_tiles.1.refs_3_, f32[3,24,384]{2,1,0:T(8,128)S(1)} %collective-permute-done.8.refs_4_, ...), custom_call_target="tpu_custom_call" | custom-call | tf_op jit(solution)/shard_map/finish/pallas_call | solution.py:368
  (5 shorter events, 0.0 us)
Async XLA Ops:
  2.0 6.0 %collective-permute-start.1 = (s32[89]{0:T(128)S(1)}, s32[89]{0:T(128)S(1)}, u32[]{:S(2)}, u32[]{:S(2)}) collective-permute-start(s32[89]{0:T(128)S(1)} %pad_add_fusion.2), channel_id=1, source_target_pairs={{0,4},{4,8},{8,12},{12,0},{1,5},{5,9},{9,13},{13,1},{2,6},{6,10},{... | collective-permute-start | bytes 1076 | tf_op jit(solution)/shard_map/ppermute | solution.py:290
  2.2 5.7 %collective-permute-start.2 = (s32[89]{0:T(128)S(1)}, s32[89]{0:T(128)S(1)}, u32[]{:S(2)}, u32[]{:S(2)}) collective-permute-start(s32[89]{0:T(128)S(1)} %pad_add_fusion.2), channel_id=1, source_target_pairs={{0,8},{4,12},{8,0},{12,4},{1,9},{5,13},{9,1},{13,5},{2,10},{6,14},... | collective-permute-start | bytes 1076 | tf_op jit(solution)/shard_map/ppermute | solution.py:290
  3.9 5.3 %collective-permute-start.3 = (s32[89]{0:T(128)S(1)}, s32[89]{0:T(128)S(1)}, u32[]{:S(2)}, u32[]{:S(2)}) collective-permute-start(s32[89]{0:T(128)S(1)} %pad_add_fusion.2), channel_id=1, source_target_pairs={{0,12},{4,0},{8,4},{12,8},{1,13},{5,1},{9,5},{13,9},{2,14},{6,2},{... | collective-permute-start | bytes 1076 | tf_op jit(solution)/shard_map/ppermute | solution.py:290
  4.5 1.0 %copy-start.4 = (f32[64,3,384]{2,0,1:T(8,128)S(1)}, f32[64,3,384]{2,0,1:T(8,128)}, u32[]{:S(2)}) copy-start(f32[64,3,384]{2,0,1:T(8,128)} %param.9) | copy-start | bytes 884740
  5.4 0.7 %copy-start.5 = (s32[64]{0:T(128)S(1)}, s32[64]{0:T(128)}, u32[]{:S(2)}) copy-start(s32[64]{0:T(128)} %refs_1_.1) | copy-start | bytes 772
  9.3 1.3 %copy-start = (f32[128,3,768]{2,0,1:T(8,128)S(1)}, f32[128,3,768]{2,0,1:T(8,128)}, u32[]{:S(2)}) copy-start(f32[128,3,768]{2,0,1:T(8,128)} %param.7) | copy-start | bytes 3538948
  10.6 1.3 %copy-start.2 = (f32[128,3,768]{2,0,1:T(8,128)S(1)}, f32[128,3,768]{2,0,1:T(8,128)}, u32[]{:S(2)}) copy-start(f32[128,3,768]{2,0,1:T(8,128)} %param.8) | copy-start | bytes 3538948
  11.8 7.4 %copy-start.1 = (f32[128,3,768]{2,0,1:T(8,128)S(1)}, f32[128,3,768]{2,0,1:T(8,128)}, u32[]{:S(2)}) copy-start(f32[128,3,768]{2,0,1:T(8,128)} %param.7) | copy-start | bytes 3538948
  11.8 7.4 %copy-start.3 = (f32[128,3,768]{2,0,1:T(8,128)S(1)}, f32[128,3,768]{2,0,1:T(8,128)}, u32[]{:S(2)}) copy-start(f32[128,3,768]{2,0,1:T(8,128)} %param.8) | copy-start | bytes 3538948
  11.8 7.4 %copy-start.6 = (s32[24]{0:T(128)S(1)}, s32[24]{0:T(128)}, u32[]{:S(2)}) copy-start(s32[24]{0:T(128)} %source_ref.3) | copy-start | bytes 292
  11.8 7.4 %copy-start.7 = (s32[24]{0:T(128)S(1)}, s32[24]{0:T(128)}, u32[]{:S(2)}) copy-start(s32[24]{0:T(128)} %target_ref.3) | copy-start | bytes 292
  13.3 13.4 %collective-permute-start.4 = (f32[6,24,384]{2,1,0:T(8,128)S(1)}, f32[6,24,384]{2,1,0:T(8,128)S(1)}, u32[]{:S(2)}, u32[]{:S(2)}) collective-permute-start(f32[6,24,384]{2,1,0:T(8,128)S(1)} %get-tuple-element.15), channel_id=1, source_target_pairs={{0,4},{4,8},{8,12},{1,5},{5,9},{9,13},{2,6},{6,10},{10,14},{3,7},{... | collective-permute-start | bytes 663560 | tf_op jit(solution)/shard_map/ppermute | solution.py:320
  14.6 12.2 %collective-permute-start.6 = (f32[6,24,384]{2,1,0:T(8,128)S(1)}, f32[6,24,384]{2,1,0:T(8,128)S(1)}, u32[]{:S(2)}, u32[]{:S(2)}) collective-permute-start(f32[6,24,384]{2,1,0:T(8,128)S(1)} %get-tuple-element.16), channel_id=1, source_target_pairs={{4,0},{8,4},{12,8},{5,1},{9,5},{13,9},{6,2},{10,6},{14,10},{7,3},{... | collective-permute-start | bytes 663560 | tf_op jit(solution)/shard_map/ppermute | solution.py:321
  26.7 4.6 %collective-permute-start.5 = (f32[6,24,384]{2,1,0:T(8,128)S(1)}, f32[6,24,384]{2,1,0:T(8,128)S(1)}, u32[]{:S(2)}, u32[]{:S(2)}) collective-permute-start(f32[6,24,384]{2,1,0:T(8,128)S(1)} %collective-permute-done.4.lefta), channel_id=1, source_target_pairs={{0,1},{1,0},{2,3},{3,2},{4,5},{5,4},{6,7},{7,6},{8,9},{9,8},{10,11... | collective-permute-start | bytes 663560 | tf_op jit(solution)/shard_map/ppermute | solution.py:290
  26.8 4.5 %collective-permute-start.7 = (f32[6,24,384]{2,1,0:T(8,128)S(1)}, f32[6,24,384]{2,1,0:T(8,128)S(1)}, u32[]{:S(2)}, u32[]{:S(2)}) collective-permute-start(f32[6,24,384]{2,1,0:T(8,128)S(1)} %collective-permute-done.6.righta), channel_id=1, source_target_pairs={{0,1},{1,0},{2,3},{3,2},{4,5},{5,4},{6,7},{7,6},{8,9},{9,8},{10,11... | collective-permute-start | bytes 663560 | tf_op jit(solution)/shard_map/ppermute | solution.py:290
  27.3 16.0 %collective-permute-start.10 = (f32[3,16,384]{2,1,0:T(8,128)S(1)}, f32[3,16,384]{2,1,0:T(8,128)S(1)}, u32[]{:S(2)}, u32[]{:S(2)}) collective-permute-start(f32[3,16,384]{2,1,0:T(8,128)S(1)} %get-tuple-element.25), channel_id=1, source_target_pairs={{0,8},{4,12},{8,0},{12,4},{1,9},{5,13},{9,1},{13,5},{2,10},{6,14},... | collective-permute-start | bytes 221192 | tf_op jit(solution)/shard_map/ppermute | solution.py:290
  27.4 16.0 %collective-permute-start.11 = (f32[3,16,384]{2,1,0:T(8,128)S(1)}, f32[3,16,384]{2,1,0:T(8,128)S(1)}, u32[]{:S(2)}, u32[]{:S(2)}) collective-permute-start(f32[3,16,384]{2,1,0:T(8,128)S(1)} %get-tuple-element.24), channel_id=1, source_target_pairs={{0,12},{4,0},{8,4},{12,8},{1,13},{5,1},{9,5},{13,9},{2,14},{6,2},{... | collective-permute-start | bytes 221192 | tf_op jit(solution)/shard_map/ppermute | solution.py:290
  27.5 15.9 %collective-permute-start.9 = (f32[3,16,384]{2,1,0:T(8,128)S(1)}, f32[3,16,384]{2,1,0:T(8,128)S(1)}, u32[]{:S(2)}, u32[]{:S(2)}) collective-permute-start(f32[3,16,384]{2,1,0:T(8,128)S(1)} %get-tuple-element.26), channel_id=1, source_target_pairs={{0,4},{4,8},{8,12},{12,0},{1,5},{5,9},{9,13},{13,1},{2,6},{6,10},{... | collective-permute-start | bytes 221192 | tf_op jit(solution)/shard_map/ppermute | solution.py:290
  41.0 5.5 %collective-permute-start.8 = (f32[3,24,384]{2,1,0:T(8,128)S(1)}, f32[3,24,384]{2,1,0:T(8,128)S(1)}, u32[]{:S(2)}, u32[]{:S(2)}) collective-permute-start(f32[3,24,384]{2,1,0:T(8,128)S(1)} %near_tiles.1.refs_3_), channel_id=1, source_target_pairs={{0,2},{2,0},{1,3},{3,1},{4,6},{6,4},{5,7},{7,5},{8,10},{10,8},{9,1... | collective-permute-start | bytes 331784 | tf_op jit(solution)/shard_map/ppermute | solution.py:290
  41.1 5.3 %collective-permute-start = (s32[25]{0:T(128)S(1)}, s32[25]{0:T(128)S(1)}, u32[]{:S(2)}, u32[]{:S(2)}) collective-permute-start(s32[25]{0:T(128)S(1)} %pad_add_fusion.1.refs_1_), channel_id=1, source_target_pairs={{0,2},{2,0},{1,3},{3,1},{4,6},{6,4},{5,7},{7,5},{8,10},{10,8},{9,1... | collective-permute-start | bytes 308 | tf_op jit(solution)/shard_map/ppermute | solution.py:290
where the time goes:
time: 48.8 us; the launch traced here: 48.7 us
  Pallas kernels  25.8 us (53%)
  starting transfers between devices  14.8 us (30%)
  local copies, waits for them, and re-layouts  4.4 us (9%)
  between operations  1.46 us (3%)
  waiting for transfers between devices  1.3 us (3%)
  other arithmetic  0.9 us (2%)
    pallas_call x1, Pallas kernels, local(): pl.pallas_call(near_tiles_kernel, out_shape=tiles, in_specs=[SMEM] * 4 +...  9.68 us
    ppermute x10, starting transfers between devices, shifted(): lax.ppermute(value, axis, [(i, (i + shift) % count) for i in range(count)])  8.94 us
    pallas_call x1, Pallas kernels, local(): pl.pallas_call(own_tiles_kernel, out_shape=tiles, in_specs=[SMEM] * 4 + [...  7.45 us
    ppermute x1, starting transfers between devices, local(): from_right = lax.ppermute(to_left, 'patch', [(b, a) for a, b in up])  4.56 us
    unnamed x16, local copies, waits for them, and re-layouts  4.17 us
    pallas_call x1, Pallas kernels, local(): pl.pallas_call(functools.partial(base_kernel, patches), out_shape=out, in...  3.1 us
    pallas_call x1, Pallas kernels, local(): pl.pallas_call(functools.partial(finish_kernel, subs, slots), out_shape=(...  2.17 us
    pallas_call x1, Pallas kernels, local(): pl.pallas_call(functools.partial(pack_history_kernel, panels), out_shape=...  1.89 us
  transfers between devices with their start and end apart: 12, of which 1 were waited for; matrix products, arithmetic and copies ran while one was open for 1% of the time, Pallas kernels for 45%

commit v1 on v0

--- a/solution.py
+++ b/solution.py
@@ -52,7 +52,7 @@
             out_ref[rel, c, pl.ds(row, 1), :] = hist_ref[c, pl.ds(b, 1), :]
         return carry
 
-    lax.fori_loop(0, hist_ref.shape[1], one, 0)
+    lax.fori_loop(0, hist_ref.shape[1], one, 0, unroll=4)
 
 
 def pack_near_kernel(slots, info_ref, left_ref, right_ref, pos_ref, drive_ref, to_left, to_right):
@@ -234,14 +234,14 @@
             places[found] = b
             return found + (dests[shift][b] // panels == me).astype(jnp.int32)
 
-        found = lax.fori_loop(0, blocks, note, 0, unroll=8)
+        lax.fori_loop(0, blocks, note, 0, unroll=8)
 
         def put(r, carry, old_ref=old_ref):
             for c in range(3):
                 out_ref[c, pl.ds(places[r], 1), :] = old_ref[c, pl.ds(r, 1), :]
             return carry
 
-        lax.fori_loop(0, found, put, 0)
+        lax.fori_loop(0, old_ref.shape[1], put, 0, unroll=True)
     mine = pos_ref[:, pl.ds(first, blocks), half_at(side, half)]
     out_ref[...] = (4.0 * mine - out_ref[...]) / 3.0
 

time: 48.8 us -> 48.5 us (level)
  the two profiles are of different devices: /device:TPU:28 before, /device:TPU:0 now
where the time goes in v1:
time: 48.5 us; the launch traced here: 48 us
  Pallas kernels  22.6 us (47%)
  starting transfers between devices  17.8 us (37%)
  local copies, waits for them, and re-layouts  4.4 us (9%)
  between operations  1.44 us (3%)
  other arithmetic  0.9 us (2%)
  waiting for transfers between devices  0.82 us (2%)
    ppermute x10, starting transfers between devices, shifted(): lax.ppermute(value, axis, [(i, (i + shift) % count) for i in range(count)])  14 us
    pallas_call x1, Pallas kernels, local(): pl.pallas_call(near_tiles_kernel, out_shape=tiles, in_specs=[SMEM] * 4 +...  7.47 us
    pallas_call x1, Pallas kernels, local(): pl.pallas_call(own_tiles_kernel, out_shape=tiles, in_specs=[SMEM] * 4 + [...  7.45 us
    unnamed x16, local copies, waits for them, and re-layouts  4.17 us
    ppermute x1, starting transfers between devices, local(): from_left = lax.ppermute(to_right, 'patch', up)  2.53 us
    pallas_call x1, Pallas kernels, local(): pl.pallas_call(functools.partial(base_kernel, patches), out_shape=out, in...  2.5 us
    pallas_call x1, Pallas kernels, local(): pl.pallas_call(functools.partial(finish_kernel, subs, slots), out_shape=(...  2.14 us
    pallas_call x1, Pallas kernels, local(): pl.pallas_call(functools.partial(pack_near_kernel, slots), out_shape=(nea...  1.68 us
  transfers between devices with their start and end apart: 12, of which 1 were waited for; matrix products, arithmetic and copies ran while one was open for 1% of the time, Pallas kernels for 39%

profile of v1, /device:TPU:0, one launch (start us, length us, event | category | flops | bytes accessed | tf_op | source)
XLA Modules:
  0.0 48.0 jit_solution(17899513980845971988)
XLA Ops:
  1.3 0.7 %pad_add_fusion.2 = s32[89]{0:T(128)S(1)} fusion(s32[64]{0:T(128)} %refs_1_.1, s32[1]{0:T(128)S(6)} %copy.9.count_ref, s32[24]{0:T(128)} %source_ref.3), kind=kLoop, calls=%fused_computation.5 | loop fusion | flops 178 | bytes 712 | tf_op jit(solution)/shard_map/concatenate | solution.py:292
  2.0 3.0 %collective-permute-start.1 = (s32[89]{0:T(128)S(1)}, s32[89]{0:T(128)S(1)}, u32[]{:S(2)}, u32[]{:S(2)}) collective-permute-start(s32[89]{0:T(128)S(1)} %pad_add_fusion.2), channel_id=1, source_target_pairs={{0,4},{4,8},{8,12},{12,0},{1,5},{5,9},{9,13},{13,1},{2,6},{6,10},{... | collective-permute-start | bytes 1076 | tf_op jit(solution)/shard_map/ppermute | solution.py:290
  5.1 2.6 %collective-permute-start.2 = (s32[89]{0:T(128)S(1)}, s32[89]{0:T(128)S(1)}, u32[]{:S(2)}, u32[]{:S(2)}) collective-permute-start(s32[89]{0:T(128)S(1)} %pad_add_fusion.2), channel_id=1, source_target_pairs={{0,8},{4,12},{8,0},{12,4},{1,9},{5,13},{9,1},{13,5},{2,10},{6,14},... | collective-permute-start | bytes 1076 | tf_op jit(solution)/shard_map/ppermute | solution.py:290
  7.6 1.3 %collective-permute-start.3 = (s32[89]{0:T(128)S(1)}, s32[89]{0:T(128)S(1)}, u32[]{:S(2)}, u32[]{:S(2)}) collective-permute-start(s32[89]{0:T(128)S(1)} %pad_add_fusion.2), channel_id=1, source_target_pairs={{0,12},{4,0},{8,4},{12,8},{1,13},{5,1},{9,5},{13,9},{2,14},{6,2},{... | collective-permute-start | bytes 1076 | tf_op jit(solution)/shard_map/ppermute | solution.py:290
  9.0 0.1 pad_add_fusion.info_ref.refs_0_
  9.1 0.0 copy-start.4
  9.1 1.0 %copy-done.4 = f32[64,3,384]{2,0,1:T(8,128)S(1)} copy-done((f32[64,3,384]{2,0,1:T(8,128)S(1)}, f32[64,3,384]{2,0,1:T(8,128)}, u32[]{:S(2)}) %copy-start.4) | copy-done | bytes 294936
  10.0 0.0 copy-start.5
  10.0 0.7 %copy-done.5 = s32[64]{0:T(128)S(1)} copy-done((s32[64]{0:T(128)S(1)}, s32[64]{0:T(128)}, u32[]{:S(2)}) %copy-start.5) | copy-done | bytes 280
  10.7 1.3 %pack_history.1.refs_6_ = f32[4,3,16,384]{3,2,1,0:T(8,128)S(1)} custom-call(s32[3]{0:T(128)S(1)} %pad_add_fusion.info_ref.refs_0_, s32[64]{0:T(128)S(1)} %copy-done.5, f32[3,64,384]{2,1,0:T(8,128)S(1)} %bitcast.20), custom_call_target="tpu_custom_call" | custom-call | tf_op jit(solution)/shard_map/pack_history/pallas_call | solution.py:297
  12.0 0.0 collective-permute-done.1.left_ref
  12.0 0.0 collective-permute-done.2
  12.1 0.0 collective-permute-done.3.right_ref
  12.1 0.0 copy-start
  12.1 1.3 %copy-done = f32[128,3,768]{2,0,1:T(8,128)S(1)} copy-done((f32[128,3,768]{2,0,1:T(8,128)S(1)}, f32[128,3,768]{2,0,1:T(8,128)}, u32[]{:S(2)}) %copy-start) | copy-done | bytes 1179672
  13.3 0.0 copy-start.2
  13.3 1.3 %copy-done.2 = f32[128,3,768]{2,0,1:T(8,128)S(1)} copy-done((f32[128,3,768]{2,0,1:T(8,128)S(1)}, f32[128,3,768]{2,0,1:T(8,128)}, u32[]{:S(2)}) %copy-start.2) | copy-done | bytes 1179672
  14.6 1.7 %pack_near.1 = (f32[6,24,384]{2,1,0:T(8,128)S(1)}, f32[6,24,384]{2,1,0:T(8,128)S(1)}) custom-call(s32[3]{0:T(128)S(1)} %pad_add_fusion.info_ref.refs_0_, s32[89]{0:T(128)S(1)} %collective-permute-done.1.left_ref, s32[89]{0:T(128)S(1)} %collective-permute-done.3.right_ref, f32[3,128,768]{2,1,0:T(8,128)S(1)} %bitcast.14, f32[3,128,768]{2,1,0:T(8,128)S(1)} %bitcast.18), custom_call_target="tpu_custom_call" | custom-call | tf_op jit(solution)/shard_map/pack_near/pallas_call | solution.py:310
  16.3 2.5 %collective-permute-start.4 = (f32[6,24,384]{2,1,0:T(8,128)S(1)}, f32[6,24,384]{2,1,0:T(8,128)S(1)}, u32[]{:S(2)}, u32[]{:S(2)}) collective-permute-start(f32[6,24,384]{2,1,0:T(8,128)S(1)} %get-tuple-element.15), channel_id=1, source_target_pairs={{0,4},{4,8},{8,12},{1,5},{5,9},{9,13},{2,6},{6,10},{10,14},{3,7},{... | collective-permute-start | bytes 663560 | tf_op jit(solution)/shard_map/ppermute | solution.py:320
  18.8 1.3 %collective-permute-start.6 = (f32[6,24,384]{2,1,0:T(8,128)S(1)}, f32[6,24,384]{2,1,0:T(8,128)S(1)}, u32[]{:S(2)}, u32[]{:S(2)}) collective-permute-start(f32[6,24,384]{2,1,0:T(8,128)S(1)} %get-tuple-element.16), channel_id=1, source_target_pairs={{4,0},{8,4},{12,8},{5,1},{9,5},{13,9},{6,2},{10,6},{14,10},{7,3},{... | collective-permute-start | bytes 663560 | tf_op jit(solution)/shard_map/ppermute | solution.py:321
  20.1 0.0 copy-done.1
  20.2 0.0 copy-done.3
  20.2 0.0 copy-done.6
  20.2 0.0 copy-done.7
  20.2 7.4 %own_tiles.1.own_ref = f32[3,24,384]{2,1,0:T(8,128)S(1)} custom-call(s32[3]{0:T(128)S(1)} %pad_add_fusion.info_ref.refs_0_, s32[24]{0:T(128)S(1)} %copy-done.6, s32[24]{0:T(128)S(1)} %copy-done.7, s32[1]{0:T(128)S(6)} %copy.9.count_ref, f32[3,128,768]{2,1,0:T(8,128)S(1)} %bitcast.15, f32[3,128,768]{2,1,0:T(8,128)S(1)} %bitcast.19), custom_call_target="tpu_custom_call" | custom-call | flops 1811939328 | bytes 2359296 | tf_op jit(solution)/shard_map/own_tiles/pallas_call | solution.py:331
  27.6 0.0 collective-permute-done.4.lefta
  27.7 0.1 collective-permute-start.5
  27.7 0.0 collective-permute-done.6.righta
  27.7 0.5 %collective-permute-start.7 = (f32[6,24,384]{2,1,0:T(8,128)S(1)}, f32[6,24,384]{2,1,0:T(8,128)S(1)}, u32[]{:S(2)}, u32[]{:S(2)}) collective-permute-start(f32[6,24,384]{2,1,0:T(8,128)S(1)} %collective-permute-done.6.righta), channel_id=1, source_target_pairs={{0,1},{1,0},{2,3},{3,2},{4,5},{5,4},{6,7},{7,6},{8,9},{9,8},{10,11... | collective-permute-start | bytes 663560 | tf_op jit(solution)/shard_map/ppermute | solution.py:290
  28.3 0.7 %collective-permute-start.10 = (f32[3,16,384]{2,1,0:T(8,128)S(1)}, f32[3,16,384]{2,1,0:T(8,128)S(1)}, u32[]{:S(2)}, u32[]{:S(2)}) collective-permute-start(f32[3,16,384]{2,1,0:T(8,128)S(1)} %get-tuple-element.25), channel_id=1, source_target_pairs={{0,8},{4,12},{8,0},{12,4},{1,9},{5,13},{9,1},{13,5},{2,10},{6,14},... | collective-permute-start | bytes 221192 | tf_op jit(solution)/shard_map/ppermute | solution.py:290
  28.9 0.9 %collective-permute-start.11 = (f32[3,16,384]{2,1,0:T(8,128)S(1)}, f32[3,16,384]{2,1,0:T(8,128)S(1)}, u32[]{:S(2)}, u32[]{:S(2)}) collective-permute-start(f32[3,16,384]{2,1,0:T(8,128)S(1)} %get-tuple-element.24), channel_id=1, source_target_pairs={{0,12},{4,0},{8,4},{12,8},{1,13},{5,1},{9,5},{13,9},{2,14},{6,2},{... | collective-permute-start | bytes 221192 | tf_op jit(solution)/shard_map/ppermute | solution.py:290
  29.8 1.1 %collective-permute-start.9 = (f32[3,16,384]{2,1,0:T(8,128)S(1)}, f32[3,16,384]{2,1,0:T(8,128)S(1)}, u32[]{:S(2)}, u32[]{:S(2)}) collective-permute-start(f32[3,16,384]{2,1,0:T(8,128)S(1)} %get-tuple-element.26), channel_id=1, source_target_pairs={{0,4},{4,8},{8,12},{12,0},{1,5},{5,9},{9,13},{13,1},{2,6},{6,10},{... | collective-permute-start | bytes 221192 | tf_op jit(solution)/shard_map/ppermute | solution.py:290
  30.9 0.0 collective-permute-done.5.leftb
  30.9 0.0 collective-permute-done.7.rightb
  30.9 7.5 %near_tiles.1.refs_3_ = f32[3,24,384]{2,1,0:T(8,128)S(1)} custom-call(s32[3]{0:T(128)S(1)} %pad_add_fusion.info_ref.refs_0_, s32[24]{0:T(128)S(1)} %copy-done.6, s32[24]{0:T(128)S(1)} %copy-done.7, s32[1]{0:T(128)S(6)} %copy.9.count_ref, f32[3,128,768]{2,1,0:T(8,128)S(1)} %bitcast.16, f32[6,24,384]{2,1,0:T(8,128)S(1)} %collective-permute-done.4.lefta, ...), custom_call_target="tpu_custom_call" | custom-call | flops 1811939328 | bytes 2359296 | tf_op jit(solution)/shard_map/near_tiles/pallas_call | solution.py:344
  38.4 3.8 %collective-permute-start.8 = (f32[3,24,384]{2,1,0:T(8,128)S(1)}, f32[3,24,384]{2,1,0:T(8,128)S(1)}, u32[]{:S(2)}, u32[]{:S(2)}) collective-permute-start(f32[3,24,384]{2,1,0:T(8,128)S(1)} %near_tiles.1.refs_3_), channel_id=1, source_target_pairs={{0,2},{2,0},{1,3},{3,1},{4,6},{6,4},{5,7},{7,5},{8,10},{10,8},{9,1... | collective-permute-start | bytes 331784 | tf_op jit(solution)/shard_map/ppermute | solution.py:290
  42.2 0.1 pad_add_fusion.1.refs_1_
  42.3 0.0 collective-permute-start
  42.3 0.1 slice.18.refs_2_
  42.4 0.1 slice.20.refs_4_
  42.4 0.1 slice.19.refs_3_
  42.5 0.0 collective-permute-done.10.refs_8_
  42.5 0.0 collective-permute-done.11.refs_9_
  42.5 0.0 collective-permute-done.9.refs_7_
  42.5 2.5 %base.1.refs_5_ = f32[3,64,384]{2,1,0:T(8,128)S(1)} custom-call(s32[3]{0:T(128)S(1)} %pad_add_fusion.info_ref.refs_0_, s32[64]{0:T(128)S(1)} %copy-done.5, s32[64]{0:T(128)S(1)} %slice.18.refs_2_, s32[64]{0:T(128)S(1)} %slice.19.refs_3_, s32[64]{0:T(128)S(1)} %slice.20.refs_4_, f32[3,128,768]{2,1,0:T(8,128)S(1)} %bitcast.17, ...), custom_call_target="tpu_custom_call" | custom-call | tf_op jit(solution)/shard_map/base/pallas_call | solution.py:359
  45.0 0.8 %collective-permute-done.refs_2_ = s32[25]{0:T(128)S(1)} collective-permute-done((s32[25]{0:T(128)S(1)}, s32[25]{0:T(128)S(1)}, u32[]{:S(2)}, u32[]{:S(2)}) %collective-permute-start) | collective-permute-done | bytes 132 | tf_op jit(solution)/shard_map/ppermute | solution.py:290
  45.8 0.0 collective-permute-done.8.refs_4_
  45.8 2.1 %finish.1 = (f32[3,64,384]{2,1,0:T(8,128)}, f32[3,64,384]{2,1,0:T(8,128)}) custom-call(s32[3]{0:T(128)S(1)} %pad_add_fusion.info_ref.refs_0_, s32[25]{0:T(128)S(1)} %pad_add_fusion.1.refs_1_, s32[25]{0:T(128)S(1)} %collective-permute-done.refs_2_, f32[3,24,384]{2,1,0:T(8,128)S(1)} %near_tiles.1.refs_3_, f32[3,24,384]{2,1,0:T(8,128)S(1)} %collective-permute-done.8.refs_4_, ...), custom_call_target="tpu_custom_call" | custom-call | tf_op jit(solution)/shard_map/finish/pallas_call | solution.py:368
  (5 shorter events, 0.0 us)
Async XLA Ops:
  2.0 10.0 %collective-permute-start.1 = (s32[89]{0:T(128)S(1)}, s32[89]{0:T(128)S(1)}, u32[]{:S(2)}, u32[]{:S(2)}) collective-permute-start(s32[89]{0:T(128)S(1)} %pad_add_fusion.2), channel_id=1, source_target_pairs={{0,4},{4,8},{8,12},{12,0},{1,5},{5,9},{9,13},{13,1},{2,6},{6,10},{... | collective-permute-start | bytes 1076 | tf_op jit(solution)/shard_map/ppermute | solution.py:290
  5.1 7.0 %collective-permute-start.2 = (s32[89]{0:T(128)S(1)}, s32[89]{0:T(128)S(1)}, u32[]{:S(2)}, u32[]{:S(2)}) collective-permute-start(s32[89]{0:T(128)S(1)} %pad_add_fusion.2), channel_id=1, source_target_pairs={{0,8},{4,12},{8,0},{12,4},{1,9},{5,13},{9,1},{13,5},{2,10},{6,14},... | collective-permute-start | bytes 1076 | tf_op jit(solution)/shard_map/ppermute | solution.py:290
  7.6 4.4 %collective-permute-start.3 = (s32[89]{0:T(128)S(1)}, s32[89]{0:T(128)S(1)}, u32[]{:S(2)}, u32[]{:S(2)}) collective-permute-start(s32[89]{0:T(128)S(1)} %pad_add_fusion.2), channel_id=1, source_target_pairs={{0,12},{4,0},{8,4},{12,8},{1,13},{5,1},{9,5},{13,9},{2,14},{6,2},{... | collective-permute-start | bytes 1076 | tf_op jit(solution)/shard_map/ppermute | solution.py:290
  9.1 1.0 %copy-start.4 = (f32[64,3,384]{2,0,1:T(8,128)S(1)}, f32[64,3,384]{2,0,1:T(8,128)}, u32[]{:S(2)}) copy-start(f32[64,3,384]{2,0,1:T(8,128)} %param.9) | copy-start | bytes 884740
  10.0 0.7 %copy-start.5 = (s32[64]{0:T(128)S(1)}, s32[64]{0:T(128)}, u32[]{:S(2)}) copy-start(s32[64]{0:T(128)} %refs_1_.1) | copy-start | bytes 772
  12.1 1.3 %copy-start = (f32[128,3,768]{2,0,1:T(8,128)S(1)}, f32[128,3,768]{2,0,1:T(8,128)}, u32[]{:S(2)}) copy-start(f32[128,3,768]{2,0,1:T(8,128)} %param.7) | copy-start | bytes 3538948
  13.3 1.3 %copy-start.2 = (f32[128,3,768]{2,0,1:T(8,128)S(1)}, f32[128,3,768]{2,0,1:T(8,128)}, u32[]{:S(2)}) copy-start(f32[128,3,768]{2,0,1:T(8,128)} %param.8) | copy-start | bytes 3538948
  14.6 5.5 %copy-start.1 = (f32[128,3,768]{2,0,1:T(8,128)S(1)}, f32[128,3,768]{2,0,1:T(8,128)}, u32[]{:S(2)}) copy-start(f32[128,3,768]{2,0,1:T(8,128)} %param.7) | copy-start | bytes 3538948
  14.6 5.5 %copy-start.3 = (f32[128,3,768]{2,0,1:T(8,128)S(1)}, f32[128,3,768]{2,0,1:T(8,128)}, u32[]{:S(2)}) copy-start(f32[128,3,768]{2,0,1:T(8,128)} %param.8) | copy-start | bytes 3538948
  14.6 5.6 %copy-start.6 = (s32[24]{0:T(128)S(1)}, s32[24]{0:T(128)}, u32[]{:S(2)}) copy-start(s32[24]{0:T(128)} %source_ref.3) | copy-start | bytes 292
  14.6 5.6 %copy-start.7 = (s32[24]{0:T(128)S(1)}, s32[24]{0:T(128)}, u32[]{:S(2)}) copy-start(s32[24]{0:T(128)} %target_ref.3) | copy-start | bytes 292
  16.3 11.3 %collective-permute-start.4 = (f32[6,24,384]{2,1,0:T(8,128)S(1)}, f32[6,24,384]{2,1,0:T(8,128)S(1)}, u32[]{:S(2)}, u32[]{:S(2)}) collective-permute-start(f32[6,24,384]{2,1,0:T(8,128)S(1)} %get-tuple-element.15), channel_id=1, source_target_pairs={{0,4},{4,8},{8,12},{1,5},{5,9},{9,13},{2,6},{6,10},{10,14},{3,7},{... | collective-permute-start | bytes 663560 | tf_op jit(solution)/shard_map/ppermute | solution.py:320
  18.8 8.9 %collective-permute-start.6 = (f32[6,24,384]{2,1,0:T(8,128)S(1)}, f32[6,24,384]{2,1,0:T(8,128)S(1)}, u32[]{:S(2)}, u32[]{:S(2)}) collective-permute-start(f32[6,24,384]{2,1,0:T(8,128)S(1)} %get-tuple-element.16), channel_id=1, source_target_pairs={{4,0},{8,4},{12,8},{5,1},{9,5},{13,9},{6,2},{10,6},{14,10},{7,3},{... | collective-permute-start | bytes 663560 | tf_op jit(solution)/shard_map/ppermute | solution.py:321
  27.7 3.3 %collective-permute-start.5 = (f32[6,24,384]{2,1,0:T(8,128)S(1)}, f32[6,24,384]{2,1,0:T(8,128)S(1)}, u32[]{:S(2)}, u32[]{:S(2)}) collective-permute-start(f32[6,24,384]{2,1,0:T(8,128)S(1)} %collective-permute-done.4.lefta), channel_id=1, source_target_pairs={{0,1},{1,0},{2,3},{3,2},{4,5},{5,4},{6,7},{7,6},{8,9},{9,8},{10,11... | collective-permute-start | bytes 663560 | tf_op jit(solution)/shard_map/ppermute | solution.py:290
  27.7 3.2 %collective-permute-start.7 = (f32[6,24,384]{2,1,0:T(8,128)S(1)}, f32[6,24,384]{2,1,0:T(8,128)S(1)}, u32[]{:S(2)}, u32[]{:S(2)}) collective-permute-start(f32[6,24,384]{2,1,0:T(8,128)S(1)} %collective-permute-done.6.righta), channel_id=1, source_target_pairs={{0,1},{1,0},{2,3},{3,2},{4,5},{5,4},{6,7},{7,6},{8,9},{9,8},{10,11... | collective-permute-start | bytes 663560 | tf_op jit(solution)/shard_map/ppermute | solution.py:290
  28.3 14.3 %collective-permute-start.10 = (f32[3,16,384]{2,1,0:T(8,128)S(1)}, f32[3,16,384]{2,1,0:T(8,128)S(1)}, u32[]{:S(2)}, u32[]{:S(2)}) collective-permute-start(f32[3,16,384]{2,1,0:T(8,128)S(1)} %get-tuple-element.25), channel_id=1, source_target_pairs={{0,8},{4,12},{8,0},{12,4},{1,9},{5,13},{9,1},{13,5},{2,10},{6,14},... | collective-permute-start | bytes 221192 | tf_op jit(solution)/shard_map/ppermute | solution.py:290
  28.9 13.6 %collective-permute-start.11 = (f32[3,16,384]{2,1,0:T(8,128)S(1)}, f32[3,16,384]{2,1,0:T(8,128)S(1)}, u32[]{:S(2)}, u32[]{:S(2)}) collective-permute-start(f32[3,16,384]{2,1,0:T(8,128)S(1)} %get-tuple-element.24), channel_id=1, source_target_pairs={{0,12},{4,0},{8,4},{12,8},{1,13},{5,1},{9,5},{13,9},{2,14},{6,2},{... | collective-permute-start | bytes 221192 | tf_op jit(solution)/shard_map/ppermute | solution.py:290
  29.8 12.7 %collective-permute-start.9 = (f32[3,16,384]{2,1,0:T(8,128)S(1)}, f32[3,16,384]{2,1,0:T(8,128)S(1)}, u32[]{:S(2)}, u32[]{:S(2)}) collective-permute-start(f32[3,16,384]{2,1,0:T(8,128)S(1)} %get-tuple-element.26), channel_id=1, source_target_pairs={{0,4},{4,8},{8,12},{12,0},{1,5},{5,9},{9,13},{13,1},{2,6},{6,10},{... | collective-permute-start | bytes 221192 | tf_op jit(solution)/shard_map/ppermute | solution.py:290
  38.4 7.4 %collective-permute-start.8 = (f32[3,24,384]{2,1,0:T(8,128)S(1)}, f32[3,24,384]{2,1,0:T(8,128)S(1)}, u32[]{:S(2)}, u32[]{:S(2)}) collective-permute-start(f32[3,24,384]{2,1,0:T(8,128)S(1)} %near_tiles.1.refs_3_), channel_id=1, source_target_pairs={{0,2},{2,0},{1,3},{3,1},{4,6},{6,4},{5,7},{7,5},{8,10},{10,8},{9,1... | collective-permute-start | bytes 331784 | tf_op jit(solution)/shard_map/ppermute | solution.py:290
  42.3 3.5 %collective-permute-start = (s32[25]{0:T(128)S(1)}, s32[25]{0:T(128)S(1)}, u32[]{:S(2)}, u32[]{:S(2)}) collective-permute-start(s32[25]{0:T(128)S(1)} %pad_add_fusion.1.refs_1_), channel_id=1, source_target_pairs={{0,2},{2,0},{1,3},{3,1},{4,6},{6,4},{5,7},{7,5},{8,10},{10,8},{9,1... | collective-permute-start | bytes 308 | tf_op jit(solution)/shard_map/ppermute | solution.py:290
